TPU v7x, 32 devices: a whole 2x2x4 slice. The times are simulated.
32 devices in a mesh: pts: 16 (over z, x, core), lab: 2 (over y).
Axes of the slice: x: 2, y: 2, z: 4, core: 2. Of those that a mesh axis runs over, the one named last changes fastest.
Arguments:
- slab_points: bfloat16 [1024, 128], P('pts'), may hold values from -6 to 6
- key_points: bfloat16 [16384, 128], P('pts'), may hold values from -6 to 6
- length_weights: float32 [128], replicated, may hold values from 0.5 to 2
- adjoint: bfloat16 [16384, 256], P('pts', 'lab'), may hold values from -2.5 to 2.5
- label_cov: float32 [256, 256], P('lab'), may hold values from -0.375 to 0.375
- cotangent: bfloat16 [1024, 256], P('pts', 'lab'), may hold values from -0.1875 to 0.1875
Outputs:
- mixed_rows: bfloat16 [1024, 256], P('pts', 'lab')
- cov_grad: float32 [256, 256], P('lab')
All inputs are finite; a program needn't handle non-finite values.
Results may differ from a plain program's by a relative error of at most 0.005.
Values may be sent and summed in bfloat16 or wider, within the bound.
A program may use at most 64 MiB of HBM per device.

v0:
```python
import jax
import jax.numpy as jnp
from jax import lax
from jax.sharding import PartitionSpec as P


def sq_norms(rows, weights):
    wide = rows.astype(jnp.float32)
    return jnp.sum(wide * wide * weights, axis=1)


def kernel_tile(slab_rows, slab_sq, scaled_keys, key_sq, width):
    inner = lax.dot_general(
        slab_rows, scaled_keys, (((1,), (1,)), ((), ())), preferred_element_type=jnp.float32
    )
    dist = slab_sq[:, None] + key_sq[None, :] - 2.0 * inner
    return jnp.exp(dist * (-2.0 / width)).astype(jnp.bfloat16)


def local(slab_points, key_points, length_weights, adjoint, label_cov, cotangent):
    width = slab_points.shape[1]
    half_labels = cotangent.shape[1]
    lab_place = lax.axis_index("lab")
    whole_slab = lax.all_gather(slab_points, "pts", axis=0, tiled=True)
    slab_sq = sq_norms(whole_slab, length_weights)
    scaled = (key_points.astype(jnp.float32) * length_weights).astype(jnp.bfloat16)
    key_sq = sq_norms(key_points, length_weights)
    full_cov = lax.all_gather(label_cov, "lab", axis=0, tiled=True)
    tile = kernel_tile(whole_slab, slab_sq, scaled, key_sq, width)
    cross_own = lax.psum_scatter(
        jnp.dot(tile, adjoint, preferred_element_type=jnp.float32),
        "pts",
        scatter_dimension=0,
        tiled=True,
    )
    cross_full, cot_full = (
        lax.all_gather(cross_own, "lab", axis=1, tiled=True),
        lax.all_gather(cotangent.astype(jnp.float32), "lab", axis=1, tiled=True),
    )
    columns = lax.dynamic_slice_in_dim(full_cov, lab_place * half_labels, half_labels, 1)
    mixed = jnp.dot(
        cross_full, columns, precision=lax.Precision.HIGHEST, preferred_element_type=jnp.float32
    ).astype(jnp.bfloat16)
    partial_grad = jnp.dot(
        cross_own.T, cot_full, precision=lax.Precision.HIGHEST, preferred_element_type=jnp.float32
    )
    grad = lax.psum(partial_grad, "pts")
    return (mixed, grad)


def solution(mesh):
    placed = (P("pts", None), P("pts", None), P(), P("pts", "lab"), P("lab", None), P("pts", "lab"))
    return jax.shard_map(
        local,
        mesh=mesh,
        in_specs=placed,
        out_specs=(P("pts", "lab"), P("lab", None)),
        check_vma=False,
    )
```

profile of v0, /device:TPU:0, one launch (start us, length us, event | category | flops | bytes accessed | tf_op | source)
XLA Modules:
  0.0 187.1 jit_solution(7596235829569515654)
XLA Ops:
  7.2 0.0 copy-start
  7.2 0.0 copy-start.1
  7.2 0.0 copy-start.4
  7.2 0.0 reduce-scatter.2.cloned.1.call-start
  7.2 24.2 %all_gather.12 = bf16[1024,128]{1,0:T(8,128)(2,1)S(1)} all-gather(bf16[64,128]{1,0:T(8,128)(2,1)} %param.6), channel_id=1, replica_groups=mesh['pts'=16,'lab'=2] {'pts'}, dimensions={0}, use_global_device_ids=true | all-gather | bytes 278528 | tf_op jit(solution)/shard_map/all_gather | solution.py:24
  31.4 1.3 multiply_reduce_fusion
  32.7 0.0 copy-done
  32.7 0.0 copy-done.1
  32.7 0.0 copy-done.4
  32.8 2.2 %fusion.3 = f32[1024,128]{1,0:T(8,128)} fusion(bf16[1024,128]{1,0:T(8,128)(2,1)S(1)} %copy-done, bf16[1024,128]{1,0:T(8,128)(2,1)S(1)} %all_gather.12, f32[1024]{0:T(1024)S(1)} %get-tuple-element.3, f32[1024]{0:T(1024)S(1)} %get-tuple-element.2, bf16[1024,128]{1,0:T(8,128)(2,1)S(1)} %copy-done.1, f32[128]{0:T(128)S(1)} %copy-done.4), kind=kOutput, calls=%fused_computation.4 | convolution fusion | flops 542507008 | bytes 1319424 | tf_op jit(solution)/shard_map/dot_general | solution.py:31
  34.9 0.0 copy-start.3
  34.9 0.0 copy-start.2
  34.9 0.0 reduce-scatter.2.cloned.1.call-update
  34.9 0.0 all-reduce.2.cloned.1.call-start
  35.0 0.6 copy-done.3
  35.6 4.6 %all_gather.15 = f32[64,256]{1,0:T(8,128)S(1)} all-gather(f32[64,128]{1,0:T(8,128)S(1)} %convert_element_type.24), channel_id=1, replica_groups=mesh['pts'=16,'lab'=2] {'lab'}, dimensions={1}, use_global_device_ids=true | all-gather | bytes 98304 | tf_op jit(solution)/shard_map/all_gather | solution.py:38
  40.2 0.0 copy-done.2
  40.2 5.6 %all_gather.14 = f32[256,256]{1,0:T(8,128)S(1)} all-gather(f32[128,256]{1,0:T(8,128)S(1)} %copy-done.2), channel_id=1, replica_groups=mesh['pts'=16,'lab'=2] {'lab'}, dimensions={0}, use_global_device_ids=true | all-gather | bytes 393216 | tf_op jit(solution)/shard_map/all_gather | solution.py:28
  45.9 42.3 %reduce-scatter.2.cloned.1.call-done = f32[64,128]{1,0:T(8,128)} async-done(((f32[1024,128]{1,0:T(8,128)}), f32[64,128]{1,0:T(8,128)}) %reduce-scatter.2.cloned.1.call-update) | async-done | bytes 32784 | tf_op jit(solution)/shard_map/reduce_scatter | solution.py:30
  88.2 1.7 fusion.15
  89.9 0.0 all-reduce.2.cloned.1.call-update
  89.9 4.8 %all_gather.13 = f32[64,256]{1,0:T(8,128)S(1)} all-gather(f32[64,128]{1,0:T(8,128)} %reduce-scatter.2.cloned.1.call-done), channel_id=1, replica_groups=mesh['pts'=16,'lab'=2] {'lab'}, dimensions={1}, use_global_device_ids=true | all-gather | bytes 98304 | tf_op jit(solution)/shard_map/all_gather | solution.py:37
  94.7 0.8 convolution_convert_fusion
  95.6 83.1 %all-reduce.2.cloned.1.call-done = f32[128,256]{1,0:T(8,128)} async-done(((f32[128,256]{1,0:T(8,128)}), f32[128,256]{1,0:T(8,128)}) %all-reduce.2.cloned.1.call-update) | async-done | bytes 131088 | tf_op jit(solution)/shard_map/psum | solution.py:47
  178.7 1.6 copy.9
  (1 shorter events, 0.0 us)
Async XLA Ops:
  7.2 25.6 %copy-start = (bf16[1024,128]{1,0:T(8,128)(2,1)S(1)}, bf16[1024,128]{1,0:T(8,128)(2,1)}, u32[]{:S(2)}) copy-start(bf16[1024,128]{1,0:T(8,128)(2,1)} %param.9) | copy-start | bytes 786436
  7.2 25.6 %copy-start.1 = (bf16[1024,128]{1,0:T(8,128)(2,1)S(1)}, bf16[1024,128]{1,0:T(8,128)(2,1)}, u32[]{:S(2)}) copy-start(bf16[1024,128]{1,0:T(8,128)(2,1)} %param.7) | copy-start | bytes 786436
  7.2 25.6 %copy-start.4 = (f32[128]{0:T(128)S(1)}, f32[128]{0:T(128)}, u32[]{:S(2)}) copy-start(f32[128]{0:T(128)} %param.8) | copy-start | bytes 1540
  7.2 81.0 %reduce-scatter.2.cloned.1.call-start = ((), (), s32[]{:S(2)}) async-start(), calls=%async_computation.1 | async-start | bytes 557056 | tf_op jit(solution)/shard_map/reduce_scatter | solution.py:30
  34.9 0.7 copy-start.3
  34.9 5.3 %copy-start.2 = (f32[128,256]{1,0:T(8,128)S(1)}, f32[128,256]{1,0:T(8,128)}, u32[]{:S(2)}) copy-start(f32[128,256]{1,0:T(8,128)} %param.10) | copy-start | bytes 393220
  34.9 143.7 %all-reduce.2.cloned.1.call-start = ((), (), s32[]{:S(2)}) async-start(), calls=%async_computation.2 | async-start | bytes 262144 | tf_op jit(solution)/shard_map/psum | solution.py:47
Sparse Core Ops, SparseCore 0:
  35.1 53.0 reduce-scatter.1
  92.6 86.0 all-reduce.1
where the time goes:
time: 188 us; the launch traced here: 187 us
  waiting for transfers between devices  125 us (66%)
  blocking collectives  39.2 us (21%)
  between operations  14.1 us (8%)
  matrix products  4.71 us (3%)
  local copies, waits for them, and re-layouts  2.23 us (1%)
    psum x1, waiting for transfers between devices, local(): grad = lax.psum(partial_grad, 'pts')  83.1 us
    reduce_scatter x1, waiting for transfers between devices, local(): lax.psum_scatter(jnp.dot(tile, adjoint, preferred_element_type=jnp.float3...  42.3 us
    all_gather x1, blocking collectives, local(): whole_slab = lax.all_gather(slab_points, 'pts', axis=0, tiled=True)  24.2 us
    all_gather x1, blocking collectives, local(): full_cov = lax.all_gather(label_cov, 'lab', axis=0, tiled=True)  5.63 us
    all_gather x1, blocking collectives, local(): lax.all_gather(cross_own, 'lab', axis=1, tiled=True)  4.8 us
    all_gather x1, blocking collectives, local(): lax.all_gather(cotangent.astype(jnp.float32), 'lab', axis=1, tiled=True)  4.58 us
  transfers between devices with their start and end apart: 2, of which 2 were waited for; matrix products, arithmetic and copies ran while one was open for 0% of the time, Pallas kernels for 0%

commit v1 on v0

v1 whole, which is shorter than its diff:
```python
import functools

import jax
import jax.numpy as jnp
from jax import lax
from jax.experimental import pallas as pl
from jax.experimental.pallas import tpu as pltpu
from jax.sharding import PartitionSpec as P

MESH = pl.DeviceIdType.MESH
HIGHEST = lax.Precision.HIGHEST
GROUP = 4
CHUNK = 16


def kernel(
    n, chunks,
    slab_hbm, key_hbm, w_hbm, adj_hbm, cov_hbm, cot_hbm,
    mixed_ref, grad_ref,
    key, w, adj, cov, cot, slab_all, part, got, mix_out, mix_in, gpart, ggot, gown, gall,
    scaled_t, key_term,
    loc, slab_send, slab_recv, part_send, part_recv, cot_send, cot_recv,
    mix_send, mix_recv, g_send, g_recv, f_send, f_recv,
):
    me = lax.axis_index("pts")
    lab = lax.axis_index("lab")
    other = 1 - lab
    groups = n // GROUP
    g_me = me // GROUP
    j_me = lax.rem(me, GROUP)
    rows, width = slab_hbm.shape
    half = adj_hbm.shape[1]
    strips = half // CHUNK

    def greet(k, c):
        pl.semaphore_signal(
            barrier, inc=1, device_id=(lax.rem(me + k, n), lab), device_id_type=MESH
        )
        return c

    barrier = pltpu.get_barrier_semaphore()
    lax.fori_loop(1, n, greet, 0)
    pl.semaphore_signal(barrier, inc=1, device_id=(me, other), device_id_type=MESH)

    loads = [
        pltpu.make_async_copy(src, dst, loc.at[i])
        for i, (src, dst) in enumerate(
            ((key_hbm, key), (w_hbm, w), (adj_hbm, adj), (cov_hbm, cov), (cot_hbm, cot.at[lab]))
        )
    ]
    for copy in loads:
        copy.start()
    pltpu.make_async_copy(slab_hbm, slab_all.at[me], slab_recv.at[g_me]).start()
    pl.semaphore_wait(barrier, n)

    def member(g, j):
        return g * GROUP + lax.rem(j_me + j, GROUP)

    def send_slab(q):
        pltpu.make_async_remote_copy(
            src_ref=slab_hbm, dst_ref=slab_all.at[me], send_sem=slab_send,
            recv_sem=slab_recv.at[g_me], device_id=(q, lab), device_id_type=MESH,
        ).start()

    for j in range(1, GROUP):
        send_slab(member(g_me, j))

    def send_group(k, c):
        g = lax.rem(g_me + groups - k, groups)
        for j in range(GROUP):
            send_slab(member(g, j))
        return c

    lax.fori_loop(1, groups, send_group, 0)
    cot_copy = pltpu.make_async_remote_copy(
        src_ref=cot_hbm, dst_ref=cot.at[lab], send_sem=cot_send, recv_sem=cot_recv,
        device_id=(me, other), device_id_type=MESH,
    )
    cot_copy.start()

    loads[0].wait()
    loads[1].wait()
    w_row = w[...]
    w_col = jnp.broadcast_to(w_row, (8, width)).T[:, :1]
    key_t = key[...].astype(jnp.float32).T
    weighted = key_t * w_col
    scaled_t[...] = weighted.astype(jnp.bfloat16)
    key_term[...] = jnp.sum(weighted * key_t, axis=0, keepdims=True) * (-2.0 / width)
    loads[2].wait()

    def partial(g):
        block = slab_all.at[pl.ds(g * GROUP, GROUP)]
        pltpu.make_async_copy(block, block, slab_recv.at[g]).wait()
        s = block[...].reshape(GROUP * rows, width)
        wide = s.astype(jnp.float32)
        s_term = jnp.sum(wide * wide * w_row, axis=1, keepdims=True) * (-2.0 / width)
        inner = jnp.dot(s, scaled_t[...], preferred_element_type=jnp.float32)
        tile = jnp.exp((s_term + key_term[...]) + inner * (4.0 / width)).astype(jnp.bfloat16)
        sums = jnp.dot(tile, adj[...], preferred_element_type=jnp.float32)
        part[pl.ds(g * GROUP, GROUP)] = sums.astype(jnp.bfloat16).reshape(GROUP, rows, half)

    def send_part(q):
        pltpu.make_async_remote_copy(
            src_ref=part.at[q], dst_ref=got.at[me], send_sem=part_send,
            recv_sem=part_recv, device_id=(q, lab), device_id_type=MESH,
        ).start()

    partial(g_me)
    pltpu.make_async_copy(part.at[me], got.at[me], part_recv).start()
    for j in range(1, GROUP):
        send_part(member(g_me, j))

    def step(k, c):
        g = lax.rem(g_me + k, groups)
        partial(g)
        for j in range(GROUP):
            send_part(member(g, j))
        return c

    lax.fori_loop(1, groups, step, 0)

    for copy in loads[3:]:
        copy.wait()
    cot_copy.wait()
    pltpu.make_async_copy(got, got, part_recv).wait()
    cross = jnp.sum(got[...].astype(jnp.float32), axis=0)

    cross_t = cross.T
    high = cross_t.astype(jnp.bfloat16)
    low = (cross_t - high.astype(jnp.float32)).astype(jnp.bfloat16)
    for h in range(2):
        c_half = cot[h]
        g_half = jnp.dot(high, c_half, preferred_element_type=jnp.float32) + jnp.dot(
            low, c_half, preferred_element_type=jnp.float32
        )
        gpart[h * strips:(h + 1) * strips] = g_half.astype(jnp.bfloat16).reshape(
            strips, CHUNK, half
        )

    def send_grad(q):
        pltpu.make_async_remote_copy(
            src_ref=gpart.at[q], dst_ref=ggot.at[me], send_sem=g_send,
            recv_sem=g_recv, device_id=(q, lab), device_id_type=MESH,
        ).start()

    def send_fin(q):
        pltpu.make_async_remote_copy(
            src_ref=gown, dst_ref=gall.at[me], send_sem=f_send,
            recv_sem=f_recv, device_id=(q, lab), device_id_type=MESH,
        ).start()

    def spread(k, c):
        send_grad(lax.rem(me + k, n))
        return c

    def spread_some(q, c):
        @pl.when(q != me)
        def _():
            send_grad(q)
        return c

    if n == chunks:
        lax.fori_loop(1, n, spread, 0)
    else:
        lax.fori_loop(0, chunks, spread_some, 0)

    def mixed_part(which):
        columns = pl.ds(pl.multiple_of(which * half, half), half)
        return jnp.dot(
            cross, cov[:, columns], precision=HIGHEST, preferred_element_type=jnp.float32
        )

    mix_out[...] = mixed_part(other)
    mix_copy = pltpu.make_async_remote_copy(
        src_ref=mix_out, dst_ref=mix_in, send_sem=mix_send, recv_sem=mix_recv,
        device_id=(me, other), device_id_type=MESH,
    )
    mix_copy.start()
    mixed_own = mixed_part(lab)

    def reduce_own():
        pltpu.make_async_copy(gpart.at[me], ggot.at[me], g_recv).start()
        pltpu.make_async_copy(ggot, ggot, g_recv).wait()
        gown[...] = jnp.sum(ggot[...].astype(jnp.float32), axis=0).astype(jnp.bfloat16)
        pltpu.make_async_copy(gown, gall.at[me], f_recv).start()

        def fan(k, c):
            send_fin(lax.rem(me + k, n))
            return c

        lax.fori_loop(1, n, fan, 0)

    if n == chunks:
        reduce_own()
    else:
        pl.when(me < chunks)(reduce_own)

    mix_copy.wait()
    mixed_ref[...] = (mixed_own + mix_in[...]).astype(jnp.bfloat16)

    pltpu.make_async_copy(gall, gall, f_recv).wait()
    for h in range(2):
        grad_ref[:, h * half:(h + 1) * half] = (
            gall[h * strips:(h + 1) * strips].reshape(half, half).astype(jnp.float32)
        )

    rest = slab_all.at[pl.ds(0, n - 1)]
    pltpu.make_async_copy(rest, rest, slab_send).wait()
    rest = part.at[pl.ds(0, n - 1)]
    pltpu.make_async_copy(rest, rest, part_send).wait()

    def drain_grad(count):
        piece = gpart.at[pl.ds(0, count)]
        pltpu.make_async_copy(piece, piece, g_send).wait()

    def drain_fin():
        sent = ggot.at[pl.ds(0, n - 1)]
        pltpu.make_async_copy(sent, sent, f_send).wait()

    if n == chunks:
        drain_grad(chunks - 1)
        drain_fin()
    else:
        @pl.when(me < chunks)
        def _():
            drain_grad(chunks - 1)
            drain_fin()

        @pl.when(me >= chunks)
        def _():
            drain_grad(chunks)


def local(n, slab_points, key_points, length_weights, adjoint, label_cov, cotangent):
    rows, width = slab_points.shape
    keys, half = adjoint.shape
    labels = label_cov.shape[1]
    chunks = (half // CHUNK) * (labels // half)
    bf16, f32 = jnp.bfloat16, jnp.float32
    dma = pltpu.SemaphoreType.DMA
    return pl.pallas_call(
        functools.partial(kernel, n, chunks),
        out_shape=(
            jax.ShapeDtypeStruct((rows, half), bf16),
            jax.ShapeDtypeStruct((half, labels), f32),
        ),
        in_specs=[pl.BlockSpec(memory_space=pl.ANY)] * 6,
        out_specs=[pl.BlockSpec(memory_space=pltpu.VMEM)] * 2,
        scratch_shapes=[
            pltpu.VMEM((keys, width), bf16),
            pltpu.VMEM((1, width), f32),
            pltpu.VMEM((keys, half), bf16),
            pltpu.VMEM((half, labels), f32),
            pltpu.VMEM((2, rows, half), bf16),
            pltpu.VMEM((n, rows, width), bf16),
            pltpu.VMEM((n, rows, half), bf16),
            pltpu.VMEM((n, rows, half), bf16),
            pltpu.VMEM((rows, half), f32),
            pltpu.VMEM((rows, half), f32),
            pltpu.VMEM((chunks, CHUNK, half), bf16),
            pltpu.VMEM((n, CHUNK, half), bf16),
            pltpu.VMEM((CHUNK, half), bf16),
            pltpu.VMEM((chunks, CHUNK, half), bf16),
            pltpu.VMEM((width, keys), bf16),
            pltpu.VMEM((1, keys), f32),
            dma((5,)),
            dma, dma((n // GROUP,)), dma, dma, dma, dma, dma, dma, dma, dma, dma, dma,
        ],
        compiler_params=pltpu.CompilerParams(
            collective_id=0, has_side_effects=True, vmem_limit_bytes=40 * 1024 * 1024
        ),
    )(slab_points, key_points, length_weights.reshape(1, width), adjoint, label_cov, cotangent)


def solution(mesh):
    placed = (P("pts", None), P("pts", None), P(), P("pts", "lab"), P("lab", None), P("pts", "lab"))
    return jax.shard_map(
        functools.partial(local, mesh.shape["pts"]),
        mesh=mesh,
        in_specs=placed,
        out_specs=(P("pts", "lab"), P("lab", None)),
        check_vma=False,
    )
```

time: 188 us -> 35.8 us (0.19)
  waiting for transfers between devices: 125 us -> 0 us
  blocking collectives: 39.2 us -> 0 us
  Pallas kernels: 0 us -> 28.7 us
  between operations: 14.1 us -> 0.65 us
  matrix products: 4.71 us -> 0 us
  local copies, waits for them, and re-layouts: 2.23 us -> 6.15 us
    psum x1 -> x0, waiting for transfers between devices: 83.1 us -> none  [local(): grad = lax.psum(partial_grad, 'pts')]
    reduce_scatter x1 -> x0, waiting for transfers between devices: 42.3 us -> none  [local(): lax.psum_scatter(jnp.dot(tile, adjoint, preferred_element_type=jnp.float3...]
    all_gather x4 -> x0, blocking collectives: 39.2 us -> none  [the longest x1 24.2 us: local(): whole_slab = lax.all_gather(slab_points, 'pts', axis=0, tiled=True)]
    pallas_call x0 -> x1, Pallas kernels: none -> 28.7 us  [local(): pl.pallas_call(functools.partial(kernel, n, chunks), out_shape=(jax.Shape...]
    dot_general x3 -> x0, matrix products: 4.71 us -> none  [the longest x1 2.16 us: local(): jnp.dot(tile, adjoint, preferred_element_type=jnp.float32)]
    unnamed x11 -> x14, local copies, waits for them, and re-layouts: 2.23 us -> 6.15 us
  transfers between devices with their start and end apart: 2 -> 0, of which waited for: 2 -> 0; matrix products, arithmetic and copies ran while one was open for 0% -> 0% of each run, Pallas kernels for 0% -> 0%
where the time goes in v1:
time: 35.8 us; the launch traced here: 35.5 us
  Pallas kernels  28.7 us (80%)
  local copies, waits for them, and re-layouts  6.15 us (17%)
  between operations  0.65 us (2%)
    pallas_call x1, Pallas kernels, local(): pl.pallas_call(functools.partial(kernel, n, chunks), out_shape=(jax.Shape...  28.7 us
    unnamed x14, local copies, waits for them, and re-layouts  6.15 us

profile of v1, /device:TPU:0, one launch (start us, length us, event | category | flops | bytes accessed | tf_op | source)
XLA Modules:
  0.0 35.5 jit_solution(1728905191440132398)
XLA Ops:
  0.6 0.0 copy-start.5
  0.6 0.6 %copy-done.5 = f32[128]{0:T(128)S(1)} copy-done((f32[128]{0:T(128)S(1)}, f32[128]{0:T(128)}, u32[]{:S(2)}) %copy-start.5) | copy-done | bytes 536
  1.3 0.0 copy-start
  1.3 0.9 %copy-done = bf16[1024,128]{1,0:T(8,128)(2,1)S(1)} copy-done((bf16[1024,128]{1,0:T(8,128)(2,1)S(1)}, bf16[1024,128]{1,0:T(8,128)(2,1)}, u32[]{:S(2)}) %copy-start) | copy-done | bytes 262168
  2.2 0.0 copy-start.1
  2.2 0.9 %copy-done.1 = bf16[1024,128]{1,0:T(8,128)(2,1)S(1)} copy-done((bf16[1024,128]{1,0:T(8,128)(2,1)S(1)}, bf16[1024,128]{1,0:T(8,128)(2,1)}, u32[]{:S(2)}) %copy-start.1) | copy-done | bytes 262168
  3.2 0.0 copy-start.2
  3.2 0.9 %copy-done.2 = f32[128,256]{1,0:T(8,128)S(1)} copy-done((f32[128,256]{1,0:T(8,128)S(1)}, f32[128,256]{1,0:T(8,128)}, u32[]{:S(2)}) %copy-start.2) | copy-done | bytes 131096
  4.1 0.0 copy-start.3
  4.1 0.7 %copy-done.3 = bf16[64,128]{1,0:T(8,128)(2,1)S(1)} copy-done((bf16[64,128]{1,0:T(8,128)(2,1)S(1)}, bf16[64,128]{1,0:T(8,128)(2,1)}, u32[]{:S(2)}) %copy-start.3) | copy-done | bytes 16408
  4.8 0.0 copy-start.4
  4.8 0.7 %copy-done.4 = bf16[64,128]{1,0:T(8,128)(2,1)S(1)} copy-done((bf16[64,128]{1,0:T(8,128)(2,1)S(1)}, bf16[64,128]{1,0:T(8,128)(2,1)}, u32[]{:S(2)}) %copy-start.4) | copy-done | bytes 16408
  5.5 28.7 %shard_map.77 = (bf16[64,128]{1,0:T(8,128)(2,1)S(1)}, f32[128,256]{1,0:T(8,128)S(1)}) custom-call(bf16[64,128]{1,0:T(8,128)(2,1)S(1)} %copy-done.3, bf16[1024,128]{1,0:T(8,128)(2,1)S(1)} %copy-done, f32[1,128]{1,0:T(1,128)S(1)} %bitcast.1, bf16[1024,128]{1,0:T(8,128)(2,1)S(1)} %copy-done.1, f32[128,256]{1,0:T(8,128)S(1)} %copy-done.2, ...), custom_call_target="tpu_custom_call" | custom-call | tf_op jit(solution)/shard_map/pallas_call | solution.py:241
  34.2 0.6 %copy.10 = bf16[64,128]{1,0:T(8,128)(2,1)} copy(bf16[64,128]{1,0:T(8,128)(2,1)S(1)} %get-tuple-element.4) | data formatting | bytes 32768
  34.8 0.7 %copy.11 = f32[128,256]{1,0:T(8,128)} copy(f32[128,256]{1,0:T(8,128)S(1)} %get-tuple-element.5) | data formatting | bytes 262144
Async XLA Ops:
  0.6 0.7 %copy-start.5 = (f32[128]{0:T(128)S(1)}, f32[128]{0:T(128)}, u32[]{:S(2)}) copy-start(f32[128]{0:T(128)} %param.8) | copy-start | bytes 1540
  1.3 0.9 %copy-start = (bf16[1024,128]{1,0:T(8,128)(2,1)S(1)}, bf16[1024,128]{1,0:T(8,128)(2,1)}, u32[]{:S(2)}) copy-start(bf16[1024,128]{1,0:T(8,128)(2,1)} %key_hbm.1) | copy-start | bytes 786436
  2.2 0.9 %copy-start.1 = (bf16[1024,128]{1,0:T(8,128)(2,1)S(1)}, bf16[1024,128]{1,0:T(8,128)(2,1)}, u32[]{:S(2)}) copy-start(bf16[1024,128]{1,0:T(8,128)(2,1)} %adj_hbm.1) | copy-start | bytes 786436
  3.2 0.9 %copy-start.2 = (f32[128,256]{1,0:T(8,128)S(1)}, f32[128,256]{1,0:T(8,128)}, u32[]{:S(2)}) copy-start(f32[128,256]{1,0:T(8,128)} %cov_hbm.1) | copy-start | bytes 393220
  4.1 0.7 %copy-start.3 = (bf16[64,128]{1,0:T(8,128)(2,1)S(1)}, bf16[64,128]{1,0:T(8,128)(2,1)}, u32[]{:S(2)}) copy-start(bf16[64,128]{1,0:T(8,128)(2,1)} %slab_hbm.1) | copy-start | bytes 49156
  4.8 0.7 %copy-start.4 = (bf16[64,128]{1,0:T(8,128)(2,1)S(1)}, bf16[64,128]{1,0:T(8,128)(2,1)}, u32[]{:S(2)}) copy-start(bf16[64,128]{1,0:T(8,128)(2,1)} %cot_hbm.1) | copy-start | bytes 49156

commit v2 on v1

--- a/solution.py
+++ b/solution.py
@@ -244,7 +244,7 @@
             jax.ShapeDtypeStruct((rows, half), bf16),
             jax.ShapeDtypeStruct((half, labels), f32),
         ),
-        in_specs=[pl.BlockSpec(memory_space=pl.ANY)] * 6,
+        in_specs=[pl.BlockSpec(memory_space=pltpu.HBM)] * 6,
         out_specs=[pl.BlockSpec(memory_space=pltpu.VMEM)] * 2,
         scratch_shapes=[
             pltpu.VMEM((keys, width), bf16),
@@ -267,7 +267,7 @@
             dma, dma((n // GROUP,)), dma, dma, dma, dma, dma, dma, dma, dma, dma, dma,
         ],
         compiler_params=pltpu.CompilerParams(
-            collective_id=0, has_side_effects=True, vmem_limit_bytes=40 * 1024 * 1024
+            collective_id=0, has_side_effects=True, vmem_limit_bytes=60 * 1024 * 1024
         ),
     )(slab_points, key_points, length_weights.reshape(1, width), adjoint, label_cov, cotangent)
 

time: 35.8 us -> 33.1 us (0.925)
  local copies, waits for them, and re-layouts: 6.15 us -> 2.89 us
  Pallas kernels: 28.7 us -> 29.3 us
    unnamed x14 -> x2, local copies, waits for them, and re-layouts: 6.15 us -> 2.89 us
    pallas_call x1, Pallas kernels: 28.7 us -> 29.3 us  [local(): pl.pallas_call(functools.partial(kernel, n, chunks), out_shape=(jax.Shape...]
where the time goes in v2:
time: 33.1 us; the launch traced here: 32.8 us
  Pallas kernels  29.3 us (89%)
  local copies, waits for them, and re-layouts  2.89 us (9%)
  between operations  0.64 us (2%)
    pallas_call x1, Pallas kernels, local(): pl.pallas_call(functools.partial(kernel, n, chunks), out_shape=(jax.Shape...  29.3 us
    unnamed x2, local copies, waits for them, and re-layouts  2.89 us

profile of v2, /device:TPU:0, one launch (start us, length us, event | category | flops | bytes accessed | tf_op | source)
XLA Modules:
  0.0 32.8 jit_solution(5112504981770858214)
XLA Ops:
  0.6 29.3 %shard_map.77 = (bf16[64,128]{1,0:T(8,128)(2,1)}, f32[128,256]{1,0:T(8,128)}) custom-call(bf16[64,128]{1,0:T(8,128)(2,1)} %slab_hbm.1, bf16[1024,128]{1,0:T(8,128)(2,1)} %key_hbm.1, f32[1,128]{1,0:T(1,128)} %bitcast.1, bf16[1024,128]{1,0:T(8,128)(2,1)} %adj_hbm.1, f32[128,256]{1,0:T(8,128)} %cov_hbm.1, bf16[64,128]{1,0:T(8,128)(2,1)} %cot_hbm.1), custom_call_target="tpu_custom_call" | custom-call | tf_op jit(solution)/shard_map/pallas_call | solution.py:241
  29.9 1.3 %copy.10 = bf16[64,128]{1,0:T(8,128)(2,1)} copy(bf16[64,128]{1,0:T(8,128)(2,1)} %get-tuple-element.4) | data formatting | bytes 32768
  31.3 1.6 %copy.11 = f32[128,256]{1,0:T(8,128)} copy(f32[128,256]{1,0:T(8,128)} %get-tuple-element.5) | data formatting | bytes 262144

commit v3 on v2

--- a/solution.py
+++ b/solution.py
@@ -9,7 +9,7 @@
 
 MESH = pl.DeviceIdType.MESH
 HIGHEST = lax.Precision.HIGHEST
-GROUP = 4
+PAIR = 2
 CHUNK = 16
 
 
@@ -17,17 +17,21 @@
     n, chunks,
     slab_hbm, key_hbm, w_hbm, adj_hbm, cov_hbm, cot_hbm,
     mixed_ref, grad_ref,
-    key, w, adj, cov, cot, slab_all, part, got, mix_out, mix_in, gpart, ggot, gown, gall,
+    key, w, adj, cov, cot, slab_all, pair_out, pair_in, kept, part, got, mix_out, mix_in, gpart, ggot, gown, gall,
     scaled_t, key_term,
-    loc, slab_send, slab_recv, part_send, part_recv, cot_send, cot_recv,
+    loc, slab_send, slab_recv, fwd_send, fwd_recv, pair_send, pair_recv, part_send, part_recv, cot_send, cot_recv,
     mix_send, mix_recv, g_send, g_recv, f_send, f_recv,
 ):
     me = lax.axis_index("pts")
     lab = lax.axis_index("lab")
     other = 1 - lab
-    groups = n // GROUP
-    g_me = me // GROUP
-    j_me = lax.rem(me, GROUP)
+    chip = me // 2
+    core = lax.rem(me, 2)
+    sibling = chip * 2 + 1 - core
+    chips = n // 2
+    groups = chips // PAIR
+    unrolled = groups <= 4
+    g_me = chip // PAIR
     rows, width = slab_hbm.shape
     half = adj_hbm.shape[1]
     strips = half // CHUNK
@@ -50,28 +54,31 @@
     ]
     for copy in loads:
         copy.start()
-    pltpu.make_async_copy(slab_hbm, slab_all.at[me], slab_recv.at[g_me]).start()
+    mine = slab_all.at[core, chip]
+    pltpu.make_async_copy(slab_hbm, mine, slab_recv.at[g_me]).start()
     pl.semaphore_wait(barrier, n)
 
+    def send_slab(q):
+        pltpu.make_async_remote_copy(
+            src_ref=slab_hbm, dst_ref=mine, send_sem=slab_send,
+            recv_sem=slab_recv.at[g_me], device_id=(q, lab), device_id_type=MESH,
+        ).start()
+
     def member(g, j):
-        return g * GROUP + lax.rem(j_me + j, GROUP)
-
-    def send_slab(q):
-        pltpu.make_async_remote_copy(
-            src_ref=slab_hbm, dst_ref=slab_all.at[me], send_sem=slab_send,
-            recv_sem=slab_recv.at[g_me], device_id=(q, lab), device_id_type=MESH,
-        ).start()
-
-    for j in range(1, GROUP):
-        send_slab(member(g_me, j))
+        return (g * PAIR + lax.rem(chip + j, PAIR)) * 2 + core
+
+    send_slab(member(g_me, 1))
+    for k in range(1, groups) if unrolled else ():
+        for j in range(PAIR):
+            send_slab(member(lax.rem(g_me + groups - k, groups), j))
 
     def send_group(k, c):
-        g = lax.rem(g_me + groups - k, groups)
-        for j in range(GROUP):
-            send_slab(member(g, j))
-        return c
-
-    lax.fori_loop(1, groups, send_group, 0)
+        for j in range(PAIR):
+            send_slab(member(lax.rem(g_me + groups - k, groups), j))
+        return c
+
+    if not unrolled:
+        lax.fori_loop(1, groups, send_group, 0)
     cot_copy = pltpu.make_async_remote_copy(
         src_ref=cot_hbm, dst_ref=cot.at[lab], send_sem=cot_send, recv_sem=cot_recv,
         device_id=(me, other), device_id_type=MESH,
@@ -86,38 +93,92 @@
     weighted = key_t * w_col
     scaled_t[...] = weighted.astype(jnp.bfloat16)
     key_term[...] = jnp.sum(weighted * key_t, axis=0, keepdims=True) * (-2.0 / width)
-    loads[2].wait()
+
+    def forward(g):
+        block = slab_all.at[core, pl.ds(g * PAIR, PAIR)]
+        pltpu.make_async_copy(block, block, slab_recv.at[g]).wait()
+        pltpu.make_async_remote_copy(
+            src_ref=block, dst_ref=block, send_sem=fwd_send, recv_sem=fwd_recv.at[g],
+            device_id=(sibling, lab), device_id_type=MESH,
+        ).start()
 
     def partial(g):
-        block = slab_all.at[pl.ds(g * GROUP, GROUP)]
-        pltpu.make_async_copy(block, block, slab_recv.at[g]).wait()
-        s = block[...].reshape(GROUP * rows, width)
+        block = slab_all.at[1 - core, pl.ds(g * PAIR, PAIR)]
+        pltpu.make_async_copy(block, block, fwd_recv.at[g]).wait()
+        own = slab_all[core, pl.ds(g * PAIR, PAIR)].reshape(PAIR * rows, width)
+        s = jnp.concatenate([own, block[...].reshape(PAIR * rows, width)], axis=0)
         wide = s.astype(jnp.float32)
         s_term = jnp.sum(wide * wide * w_row, axis=1, keepdims=True) * (-2.0 / width)
         inner = jnp.dot(s, scaled_t[...], preferred_element_type=jnp.float32)
         tile = jnp.exp((s_term + key_term[...]) + inner * (4.0 / width)).astype(jnp.bfloat16)
         sums = jnp.dot(tile, adj[...], preferred_element_type=jnp.float32)
-        part[pl.ds(g * GROUP, GROUP)] = sums.astype(jnp.bfloat16).reshape(GROUP, rows, half)
-
-    def send_part(q):
-        pltpu.make_async_remote_copy(
-            src_ref=part.at[q], dst_ref=got.at[me], send_sem=part_send,
+        pair_out[g] = sums[PAIR * rows:]
+        pltpu.make_async_remote_copy(
+            src_ref=pair_out.at[g], dst_ref=pair_in.at[g], send_sem=pair_send,
+            recv_sem=pair_recv.at[g], device_id=(sibling, lab), device_id_type=MESH,
+        ).start()
+        kept[g] = sums[:PAIR * rows]
+
+    def send_part(g, j):
+        q = member(g, j)
+        pltpu.make_async_remote_copy(
+            src_ref=part.at[q // 2], dst_ref=got.at[chip], send_sem=part_send,
             recv_sem=part_recv, device_id=(q, lab), device_id_type=MESH,
         ).start()
 
+    def collect(g):
+        arrived = pair_in.at[g]
+        pltpu.make_async_copy(arrived, arrived, pair_recv.at[g]).wait()
+        both = (kept[g] + arrived[...]).astype(jnp.bfloat16)
+        part[pl.ds(g * PAIR, PAIR)] = both.reshape(PAIR, rows, half)
+
+    def group_at(k):
+        return lax.rem(g_me + k, groups)
+
+    forward(g_me)
+    loads[2].wait()
+    forward(group_at(1))
     partial(g_me)
-    pltpu.make_async_copy(part.at[me], got.at[me], part_recv).start()
-    for j in range(1, GROUP):
-        send_part(member(g_me, j))
 
     def step(k, c):
-        g = lax.rem(g_me + k, groups)
-        partial(g)
-        for j in range(GROUP):
-            send_part(member(g, j))
-        return c
-
-    lax.fori_loop(1, groups, step, 0)
+        @pl.when(k + 1 < groups)
+        def _():
+            forward(group_at(k + 1))
+        partial(group_at(k))
+
+        @pl.when(k == 1)
+        def _():
+            collect(g_me)
+            pltpu.make_async_copy(part.at[chip], got.at[chip], part_recv).start()
+            send_part(g_me, 1)
+
+        @pl.when(k > 1)
+        def _():
+            g = group_at(k - 1)
+            collect(g)
+            for j in range(PAIR):
+                send_part(g, j)
+        return c
+
+    if unrolled:
+        for k in range(1, groups):
+            if k + 1 < groups:
+                forward(group_at(k + 1))
+            partial(group_at(k))
+            g = group_at(k - 1)
+            collect(g)
+            if k == 1:
+                pltpu.make_async_copy(part.at[chip], got.at[chip], part_recv).start()
+                send_part(g, 1)
+            else:
+                for j in range(PAIR):
+                    send_part(g, j)
+    else:
+        lax.fori_loop(1, groups, step, 0)
+    g = group_at(groups - 1)
+    collect(g)
+    for j in range(PAIR):
+        send_part(g, j)
 
     for copy in loads[3:]:
         copy.wait()
@@ -204,10 +265,12 @@
             gall[h * strips:(h + 1) * strips].reshape(half, half).astype(jnp.float32)
         )
 
-    rest = slab_all.at[pl.ds(0, n - 1)]
+    rest = slab_all.at[0, pl.ds(0, chips - 1)]
     pltpu.make_async_copy(rest, rest, slab_send).wait()
-    rest = part.at[pl.ds(0, n - 1)]
+    rest = part.at[pl.ds(0, chips - 1)]
     pltpu.make_async_copy(rest, rest, part_send).wait()
+    pltpu.make_async_copy(slab_all.at[0], slab_all.at[0], fwd_send).wait()
+    pltpu.make_async_copy(pair_out, pair_out, pair_send).wait()
 
     def drain_grad(count):
         piece = gpart.at[pl.ds(0, count)]
@@ -238,6 +301,8 @@
     chunks = (half // CHUNK) * (labels // half)
     bf16, f32 = jnp.bfloat16, jnp.float32
     dma = pltpu.SemaphoreType.DMA
+    chips = n // 2
+    groups = chips // PAIR
     return pl.pallas_call(
         functools.partial(kernel, n, chunks),
         out_shape=(
@@ -252,9 +317,12 @@
             pltpu.VMEM((keys, half), bf16),
             pltpu.VMEM((half, labels), f32),
             pltpu.VMEM((2, rows, half), bf16),
-            pltpu.VMEM((n, rows, width), bf16),
-            pltpu.VMEM((n, rows, half), bf16),
-            pltpu.VMEM((n, rows, half), bf16),
+            pltpu.VMEM((2, chips, rows, width), bf16),
+            pltpu.VMEM((groups, PAIR * rows, half), f32),
+            pltpu.VMEM((groups, PAIR * rows, half), f32),
+            pltpu.VMEM((groups, PAIR * rows, half), f32),
+            pltpu.VMEM((chips, rows, half), bf16),
+            pltpu.VMEM((chips, rows, half), bf16),
             pltpu.VMEM((rows, half), f32),
             pltpu.VMEM((rows, half), f32),
             pltpu.VMEM((chunks, CHUNK, half), bf16),
@@ -264,7 +332,7 @@
             pltpu.VMEM((width, keys), bf16),
             pltpu.VMEM((1, keys), f32),
             dma((5,)),
-            dma, dma((n // GROUP,)), dma, dma, dma, dma, dma, dma, dma, dma, dma, dma,
+            dma, dma((groups,)), dma, dma((groups,)), dma, dma((groups,)), dma, dma, dma, dma, dma, dma, dma, dma, dma, dma,
         ],
         compiler_params=pltpu.CompilerParams(
             collective_id=0, has_side_effects=True, vmem_limit_bytes=60 * 1024 * 1024

time: 33.1 us -> 31.9 us (0.964)
  Pallas kernels: 29.3 us -> 28.1 us
    pallas_call x1, Pallas kernels: 29.3 us -> 28.1 us  [local(): pl.pallas_call(functools.partial(kernel, n, chunks), out_shape=(jax.Shape...]
where the time goes in v3:
time: 31.9 us; the launch traced here: 31.7 us
  Pallas kernels  28.1 us (88%)
  local copies, waits for them, and re-layouts  2.89 us (9%)
  between operations  0.64 us (2%)
    pallas_call x1, Pallas kernels, local(): pl.pallas_call(functools.partial(kernel, n, chunks), out_shape=(jax.Shape...  28.1 us
    unnamed x2, local copies, waits for them, and re-layouts  2.89 us

profile of v3, /device:TPU:0, one launch (start us, length us, event | category | flops | bytes accessed | tf_op | source)
XLA Modules:
  0.0 31.7 jit_solution(6423798731784992217)
XLA Ops:
  0.6 28.1 %shard_map.77 = (bf16[64,128]{1,0:T(8,128)(2,1)}, f32[128,256]{1,0:T(8,128)}) custom-call(bf16[64,128]{1,0:T(8,128)(2,1)} %slab_hbm.1, bf16[1024,128]{1,0:T(8,128)(2,1)} %key_hbm.1, f32[1,128]{1,0:T(1,128)} %bitcast.1, bf16[1024,128]{1,0:T(8,128)(2,1)} %adj_hbm.1, f32[128,256]{1,0:T(8,128)} %cov_hbm.1, bf16[64,128]{1,0:T(8,128)(2,1)} %cot_hbm.1), custom_call_target="tpu_custom_call" | custom-call | tf_op jit(solution)/shard_map/pallas_call | solution.py:306
  28.8 1.3 %copy.10 = bf16[64,128]{1,0:T(8,128)(2,1)} copy(bf16[64,128]{1,0:T(8,128)(2,1)} %get-tuple-element.4) | data formatting | bytes 32768
  30.1 1.6 %copy.11 = f32[128,256]{1,0:T(8,128)} copy(f32[128,256]{1,0:T(8,128)} %get-tuple-element.5) | data formatting | bytes 262144

commit v4 on v3

--- a/solution.py
+++ b/solution.py
@@ -303,11 +303,14 @@
     dma = pltpu.SemaphoreType.DMA
     chips = n // 2
     groups = chips // PAIR
+    operands = (
+        slab_points, key_points, length_weights.reshape(1, width), adjoint, label_cov, cotangent
+    )
     return pl.pallas_call(
         functools.partial(kernel, n, chunks),
         out_shape=(
-            jax.ShapeDtypeStruct((rows, half), bf16),
-            jax.ShapeDtypeStruct((half, labels), f32),
+            pltpu.VMEM((rows, half), bf16),
+            pltpu.VMEM((half, labels), f32),
         ),
         in_specs=[pl.BlockSpec(memory_space=pltpu.HBM)] * 6,
         out_specs=[pl.BlockSpec(memory_space=pltpu.VMEM)] * 2,
@@ -335,9 +338,9 @@
             dma, dma((groups,)), dma, dma((groups,)), dma, dma((groups,)), dma, dma, dma, dma, dma, dma, dma, dma, dma, dma,
         ],
         compiler_params=pltpu.CompilerParams(
-            collective_id=0, has_side_effects=True, vmem_limit_bytes=60 * 1024 * 1024
+            collective_id=0, has_side_effects=True, vmem_limit_bytes=40 * 1024 * 1024
         ),
-    )(slab_points, key_points, length_weights.reshape(1, width), adjoint, label_cov, cotangent)
+    )(*(pltpu.with_memory_space_constraint(x, pltpu.HBM) for x in operands))
 
 
 def solution(mesh):

time: 31.9 us -> 29.5 us (0.925)
  local copies, waits for them, and re-layouts: 2.89 us -> 1.26 us
  Pallas kernels: 28.1 us -> 27.5 us
    unnamed x2, local copies, waits for them, and re-layouts: 2.89 us -> 1.26 us
    pallas_call x1, Pallas kernels: 28.1 us -> 27.5 us  [local(): pl.pallas_call(functools.partial(kernel, n, chunks), out_shape=(pltpu.VME...]
where the time goes in v4:
time: 29.5 us; the launch traced here: 29.4 us
  Pallas kernels  27.5 us (93%)
  local copies, waits for them, and re-layouts  1.26 us (4%)
  between operations  0.64 us (2%)
    pallas_call x1, Pallas kernels, local(): pl.pallas_call(functools.partial(kernel, n, chunks), out_shape=(pltpu.VME...  27.5 us
    unnamed x2, local copies, waits for them, and re-layouts  1.26 us

profile of v4, /device:TPU:0, one launch (start us, length us, event | category | flops | bytes accessed | tf_op | source)
XLA Modules:
  0.0 29.4 jit_solution(2627690825583918392)
XLA Ops:
  0.6 27.5 %shard_map.77 = (bf16[64,128]{1,0:T(8,128)(2,1)S(1)}, f32[128,256]{1,0:T(8,128)S(1)}) custom-call(bf16[64,128]{1,0:T(8,128)(2,1)} %slab_hbm.1, bf16[1024,128]{1,0:T(8,128)(2,1)} %key_hbm.1, f32[1,128]{1,0:T(1,128)} %bitcast.1, bf16[1024,128]{1,0:T(8,128)(2,1)} %adj_hbm.1, f32[128,256]{1,0:T(8,128)} %cov_hbm.1, bf16[64,128]{1,0:T(8,128)(2,1)} %cot_hbm.1), custom_call_target="tpu_custom_call" | custom-call | tf_op jit(solution)/shard_map/pallas_call | solution.py:309
  28.1 0.6 %copy.10 = bf16[64,128]{1,0:T(8,128)(2,1)} copy(bf16[64,128]{1,0:T(8,128)(2,1)S(1)} %get-tuple-element.2) | data formatting | bytes 32768
  28.7 0.7 %copy.11 = f32[128,256]{1,0:T(8,128)} copy(f32[128,256]{1,0:T(8,128)S(1)} %get-tuple-element.3) | data formatting | bytes 262144

commit v5 on v4

--- a/solution.py
+++ b/solution.py
@@ -17,9 +17,9 @@
     n, chunks,
     slab_hbm, key_hbm, w_hbm, adj_hbm, cov_hbm, cot_hbm,
     mixed_ref, grad_ref,
-    key, w, adj, cov, cot, slab_all, pair_out, pair_in, kept, part, got, mix_out, mix_in, gpart, ggot, gown, gall,
+    key, w, adj, cov, cot, slab_all, pair_out, pair_in, kept, part, got, mix_out, mix_in, gpart, ggot, gall,
     scaled_t, key_term,
-    loc, slab_send, slab_recv, fwd_send, fwd_recv, pair_send, pair_recv, part_send, part_recv, cot_send, cot_recv,
+    loc, slab_loc, slab_send, slab_recv, fwd_send, fwd_recv, pair_send, pair_recv, part_send, part_recv, cot_send, cot_recv,
     mix_send, mix_recv, g_send, g_recv, f_send, f_recv,
 ):
     me = lax.axis_index("pts")
@@ -30,7 +30,6 @@
     sibling = chip * 2 + 1 - core
     chips = n // 2
     groups = chips // PAIR
-    unrolled = groups <= 4
     g_me = chip // PAIR
     rows, width = slab_hbm.shape
     half = adj_hbm.shape[1]
@@ -42,6 +41,9 @@
         )
         return c
 
+    mine = slab_all.at[core, chip]
+    slab_load = pltpu.make_async_copy(slab_hbm, mine, slab_loc)
+    slab_load.start()
     barrier = pltpu.get_barrier_semaphore()
     lax.fori_loop(1, n, greet, 0)
     pl.semaphore_signal(barrier, inc=1, device_id=(me, other), device_id_type=MESH)
@@ -54,31 +56,33 @@
     ]
     for copy in loads:
         copy.start()
-    mine = slab_all.at[core, chip]
-    pltpu.make_async_copy(slab_hbm, mine, slab_recv.at[g_me]).start()
+    slab_load.wait()
     pl.semaphore_wait(barrier, n)
 
     def send_slab(q):
         pltpu.make_async_remote_copy(
-            src_ref=slab_hbm, dst_ref=mine, send_sem=slab_send,
+            src_ref=mine, dst_ref=mine, send_sem=slab_send,
             recv_sem=slab_recv.at[g_me], device_id=(q, lab), device_id_type=MESH,
         ).start()
 
     def member(g, j):
         return (g * PAIR + lax.rem(chip + j, PAIR)) * 2 + core
 
+    def to_sibling(block, g):
+        pltpu.make_async_remote_copy(
+            src_ref=block, dst_ref=block, send_sem=fwd_send, recv_sem=fwd_recv.at[g],
+            device_id=(sibling, lab), device_id_type=MESH,
+        ).start()
+
     send_slab(member(g_me, 1))
-    for k in range(1, groups) if unrolled else ():
-        for j in range(PAIR):
-            send_slab(member(lax.rem(g_me + groups - k, groups), j))
+    to_sibling(mine, g_me)
 
     def send_group(k, c):
         for j in range(PAIR):
             send_slab(member(lax.rem(g_me + groups - k, groups), j))
         return c
 
-    if not unrolled:
-        lax.fori_loop(1, groups, send_group, 0)
+    lax.fori_loop(1, groups, send_group, 0)
     cot_copy = pltpu.make_async_remote_copy(
         src_ref=cot_hbm, dst_ref=cot.at[lab], send_sem=cot_send, recv_sem=cot_recv,
         device_id=(me, other), device_id_type=MESH,
@@ -97,10 +101,7 @@
     def forward(g):
         block = slab_all.at[core, pl.ds(g * PAIR, PAIR)]
         pltpu.make_async_copy(block, block, slab_recv.at[g]).wait()
-        pltpu.make_async_remote_copy(
-            src_ref=block, dst_ref=block, send_sem=fwd_send, recv_sem=fwd_recv.at[g],
-            device_id=(sibling, lab), device_id_type=MESH,
-        ).start()
+        to_sibling(block, g)
 
     def partial(g):
         block = slab_all.at[1 - core, pl.ds(g * PAIR, PAIR)]
@@ -135,46 +136,35 @@
     def group_at(k):
         return lax.rem(g_me + k, groups)
 
-    forward(g_me)
+    near = slab_all.at[core, g_me * PAIR + lax.rem(chip + 1, PAIR)]
+    pltpu.make_async_copy(near, near, slab_recv.at[g_me]).wait()
+    to_sibling(near, g_me)
     loads[2].wait()
-    forward(group_at(1))
-    partial(g_me)
 
     def step(k, c):
         @pl.when(k + 1 < groups)
         def _():
             forward(group_at(k + 1))
+
         partial(group_at(k))
 
-        @pl.when(k == 1)
-        def _():
-            collect(g_me)
-            pltpu.make_async_copy(part.at[chip], got.at[chip], part_recv).start()
-            send_part(g_me, 1)
-
-        @pl.when(k > 1)
+        @pl.when(k > 0)
         def _():
             g = group_at(k - 1)
             collect(g)
-            for j in range(PAIR):
-                send_part(g, j)
-        return c
-
-    if unrolled:
-        for k in range(1, groups):
-            if k + 1 < groups:
-                forward(group_at(k + 1))
-            partial(group_at(k))
-            g = group_at(k - 1)
-            collect(g)
-            if k == 1:
+
+            @pl.when(k == 1)
+            def _():
                 pltpu.make_async_copy(part.at[chip], got.at[chip], part_recv).start()
-                send_part(g, 1)
-            else:
-                for j in range(PAIR):
-                    send_part(g, j)
-    else:
-        lax.fori_loop(1, groups, step, 0)
+
+            @pl.when(k > 1)
+            def _():
+                send_part(g, 0)
+
+            send_part(g, 1)
+        return c
+
+    lax.fori_loop(0, groups, step, 0)
     g = group_at(groups - 1)
     collect(g)
     for j in range(PAIR):
@@ -206,7 +196,7 @@
 
     def send_fin(q):
         pltpu.make_async_remote_copy(
-            src_ref=gown, dst_ref=gall.at[me], send_sem=f_send,
+            src_ref=gall.at[me], dst_ref=gall.at[me], send_sem=f_send,
             recv_sem=f_recv, device_id=(q, lab), device_id_type=MESH,
         ).start()
 
@@ -220,10 +210,15 @@
             send_grad(q)
         return c
 
+    def keep_grad():
+        pltpu.make_async_copy(gpart.at[me], ggot.at[me], g_recv).start()
+
     if n == chunks:
         lax.fori_loop(1, n, spread, 0)
+        keep_grad()
     else:
         lax.fori_loop(0, chunks, spread_some, 0)
+        pl.when(me < chunks)(keep_grad)
 
     def mixed_part(which):
         columns = pl.ds(pl.multiple_of(which * half, half), half)
@@ -240,10 +235,8 @@
     mixed_own = mixed_part(lab)
 
     def reduce_own():
-        pltpu.make_async_copy(gpart.at[me], ggot.at[me], g_recv).start()
         pltpu.make_async_copy(ggot, ggot, g_recv).wait()
-        gown[...] = jnp.sum(ggot[...].astype(jnp.float32), axis=0).astype(jnp.bfloat16)
-        pltpu.make_async_copy(gown, gall.at[me], f_recv).start()
+        gall[me] = jnp.sum(ggot[...].astype(jnp.float32), axis=0).astype(jnp.bfloat16)
 
         def fan(k, c):
             send_fin(lax.rem(me + k, n))
@@ -259,7 +252,15 @@
     mix_copy.wait()
     mixed_ref[...] = (mixed_own + mix_in[...]).astype(jnp.bfloat16)
 
-    pltpu.make_async_copy(gall, gall, f_recv).wait()
+    def await_grad(count):
+        pieces = gall.at[pl.ds(0, count)]
+        pltpu.make_async_copy(pieces, pieces, f_recv).wait()
+
+    if n == chunks:
+        await_grad(chunks - 1)
+    else:
+        pl.when(me < chunks)(lambda: await_grad(chunks - 1))
+        pl.when(me >= chunks)(lambda: await_grad(chunks))
     for h in range(2):
         grad_ref[:, h * half:(h + 1) * half] = (
             gall[h * strips:(h + 1) * strips].reshape(half, half).astype(jnp.float32)
@@ -330,11 +331,10 @@
             pltpu.VMEM((rows, half), f32),
             pltpu.VMEM((chunks, CHUNK, half), bf16),
             pltpu.VMEM((n, CHUNK, half), bf16),
-            pltpu.VMEM((CHUNK, half), bf16),
             pltpu.VMEM((chunks, CHUNK, half), bf16),
             pltpu.VMEM((width, keys), bf16),
             pltpu.VMEM((1, keys), f32),
-            dma((5,)),
+            dma((5,)), dma,
             dma, dma((groups,)), dma, dma((groups,)), dma, dma((groups,)), dma, dma, dma, dma, dma, dma, dma, dma, dma, dma,
         ],
         compiler_params=pltpu.CompilerParams(

time: 29.5 us -> 29.4 us (level)
  Pallas kernels: 27.5 us -> 27.2 us
where the time goes in v5:
time: 29.4 us; the launch traced here: 29.1 us
  Pallas kernels  27.2 us (93%)
  local copies, waits for them, and re-layouts  1.26 us (4%)
  between operations  0.64 us (2%)
    pallas_call x1, Pallas kernels, local(): pl.pallas_call(functools.partial(kernel, n, chunks), out_shape=(pltpu.VME...  27.2 us
    unnamed x2, local copies, waits for them, and re-layouts  1.26 us

profile of v5, /device:TPU:0, one launch (start us, length us, event | category | flops | bytes accessed | tf_op | source)
XLA Modules:
  0.0 29.1 jit_solution(16339763331549003973)
XLA Ops:
  0.6 27.2 %shard_map.77 = (bf16[64,128]{1,0:T(8,128)(2,1)S(1)}, f32[128,256]{1,0:T(8,128)S(1)}) custom-call(bf16[64,128]{1,0:T(8,128)(2,1)} %slab_hbm.1, bf16[1024,128]{1,0:T(8,128)(2,1)} %key_hbm.1, f32[1,128]{1,0:T(1,128)} %bitcast.1, bf16[1024,128]{1,0:T(8,128)(2,1)} %adj_hbm.1, f32[128,256]{1,0:T(8,128)} %cov_hbm.1, bf16[64,128]{1,0:T(8,128)(2,1)} %cot_hbm.1), custom_call_target="tpu_custom_call" | custom-call | tf_op jit(solution)/shard_map/pallas_call | solution.py:310
  27.9 0.6 %copy.10 = bf16[64,128]{1,0:T(8,128)(2,1)} copy(bf16[64,128]{1,0:T(8,128)(2,1)S(1)} %get-tuple-element.2) | data formatting | bytes 32768
  28.5 0.7 %copy.11 = f32[128,256]{1,0:T(8,128)} copy(f32[128,256]{1,0:T(8,128)S(1)} %get-tuple-element.3) | data formatting | bytes 262144

commit v6 on v5

--- a/solution.py
+++ b/solution.py
@@ -19,7 +19,8 @@
     mixed_ref, grad_ref,
     key, w, adj, cov, cot, slab_all, pair_out, pair_in, kept, part, got, mix_out, mix_in, gpart, ggot, gall,
     scaled_t, key_term,
-    loc, slab_loc, slab_send, slab_recv, fwd_send, fwd_recv, pair_send, pair_recv, part_send, part_recv, cot_send, cot_recv,
+    loc, slab_loc, slab_send, slab_recv, fwd_send, fwd_recv, pair_send, pair_recv, part_send, part_recv,
+    cot_send, cot_recv, cot_pair_send, cot_pair_recv,
     mix_send, mix_recv, g_send, g_recv, f_send, f_recv,
 ):
     me = lax.axis_index("pts")
@@ -51,7 +52,7 @@
     loads = [
         pltpu.make_async_copy(src, dst, loc.at[i])
         for i, (src, dst) in enumerate(
-            ((key_hbm, key), (w_hbm, w), (adj_hbm, adj), (cov_hbm, cov), (cot_hbm, cot.at[lab]))
+            ((key_hbm, key), (w_hbm, w), (adj_hbm, adj), (cov_hbm, cov), (cot_hbm, cot.at[lab, chip]))
         )
     ]
     for copy in loads:
@@ -83,11 +84,26 @@
         return c
 
     lax.fori_loop(1, groups, send_group, 0)
+
+    def send_cot(q):
+        own = cot.at[lab, chip]
+        pltpu.make_async_remote_copy(
+            src_ref=own, dst_ref=own, send_sem=cot_send, recv_sem=cot_recv,
+            device_id=(q, lab), device_id_type=MESH,
+        ).start()
+
+    def send_cots(k, c):
+        for j in range(PAIR):
+            send_cot(member(lax.rem(g_me + groups - k, groups), j))
+        return c
+
+    loads[4].wait()
+    send_cot(member(g_me, 1))
+    lax.fori_loop(1, groups, send_cots, 0)
     cot_copy = pltpu.make_async_remote_copy(
-        src_ref=cot_hbm, dst_ref=cot.at[lab], send_sem=cot_send, recv_sem=cot_recv,
-        device_id=(me, other), device_id_type=MESH,
+        src_ref=cot.at[lab], dst_ref=cot.at[lab], send_sem=cot_pair_send,
+        recv_sem=cot_pair_recv, device_id=(me, other), device_id_type=MESH,
     )
-    cot_copy.start()
 
     loads[0].wait()
     loads[1].wait()
@@ -156,6 +172,9 @@
             @pl.when(k == 1)
             def _():
                 pltpu.make_async_copy(part.at[chip], got.at[chip], part_recv).start()
+                arrived = cot.at[lab, pl.ds(0, chips - 1)]
+                pltpu.make_async_copy(arrived, arrived, cot_recv).wait()
+                cot_copy.start()
 
             @pl.when(k > 1)
             def _():
@@ -170,19 +189,11 @@
     for j in range(PAIR):
         send_part(g, j)
 
-    for copy in loads[3:]:
-        copy.wait()
     cot_copy.wait()
-    pltpu.make_async_copy(got, got, part_recv).wait()
-    cross = jnp.sum(got[...].astype(jnp.float32), axis=0)
-
-    cross_t = cross.T
-    high = cross_t.astype(jnp.bfloat16)
-    low = (cross_t - high.astype(jnp.float32)).astype(jnp.bfloat16)
+    sums_t = part[...].reshape(chips * rows, half).astype(jnp.float32).T.astype(jnp.bfloat16)
     for h in range(2):
-        c_half = cot[h]
-        g_half = jnp.dot(high, c_half, preferred_element_type=jnp.float32) + jnp.dot(
-            low, c_half, preferred_element_type=jnp.float32
+        g_half = jnp.dot(
+            sums_t, cot[h].reshape(chips * rows, half), preferred_element_type=jnp.float32
         )
         gpart[h * strips:(h + 1) * strips] = g_half.astype(jnp.bfloat16).reshape(
             strips, CHUNK, half
@@ -220,6 +231,10 @@
         lax.fori_loop(0, chunks, spread_some, 0)
         pl.when(me < chunks)(keep_grad)
 
+    loads[3].wait()
+    pltpu.make_async_copy(got, got, part_recv).wait()
+    cross = jnp.sum(got[...].astype(jnp.float32), axis=0)
+
     def mixed_part(which):
         columns = pl.ds(pl.multiple_of(which * half, half), half)
         return jnp.dot(
@@ -232,7 +247,6 @@
         device_id=(me, other), device_id_type=MESH,
     )
     mix_copy.start()
-    mixed_own = mixed_part(lab)
 
     def reduce_own():
         pltpu.make_async_copy(ggot, ggot, g_recv).wait()
@@ -249,6 +263,7 @@
     else:
         pl.when(me < chunks)(reduce_own)
 
+    mixed_own = mixed_part(lab)
     mix_copy.wait()
     mixed_ref[...] = (mixed_own + mix_in[...]).astype(jnp.bfloat16)
 
@@ -270,6 +285,7 @@
     pltpu.make_async_copy(rest, rest, slab_send).wait()
     rest = part.at[pl.ds(0, chips - 1)]
     pltpu.make_async_copy(rest, rest, part_send).wait()
+    pltpu.make_async_copy(rest, rest, cot_send).wait()
     pltpu.make_async_copy(slab_all.at[0], slab_all.at[0], fwd_send).wait()
     pltpu.make_async_copy(pair_out, pair_out, pair_send).wait()
 
@@ -320,7 +336,7 @@
             pltpu.VMEM((1, width), f32),
             pltpu.VMEM((keys, half), bf16),
             pltpu.VMEM((half, labels), f32),
-            pltpu.VMEM((2, rows, half), bf16),
+            pltpu.VMEM((2, chips, rows, half), bf16),
             pltpu.VMEM((2, chips, rows, width), bf16),
             pltpu.VMEM((groups, PAIR * rows, half), f32),
             pltpu.VMEM((groups, PAIR * rows, half), f32),
@@ -335,7 +351,8 @@
             pltpu.VMEM((width, keys), bf16),
             pltpu.VMEM((1, keys), f32),
             dma((5,)), dma,
-            dma, dma((groups,)), dma, dma((groups,)), dma, dma((groups,)), dma, dma, dma, dma, dma, dma, dma, dma, dma, dma,
+            dma, dma((groups,)), dma, dma((groups,)), dma, dma((groups,)),
+            *([dma] * 12),
         ],
         compiler_params=pltpu.CompilerParams(
             collective_id=0, has_side_effects=True, vmem_limit_bytes=40 * 1024 * 1024

time: 29.4 us -> 29.3 us (level)
  no operation moved by 1% of the time
where the time goes in v6:
time: 29.3 us; the launch traced here: 29 us
  Pallas kernels  27.1 us (92%)
  local copies, waits for them, and re-layouts  1.26 us (4%)
  between operations  0.64 us (2%)
    pallas_call x1, Pallas kernels, local(): pl.pallas_call(functools.partial(kernel, n, chunks), out_shape=(pltpu.VME...  27.1 us
    unnamed x2, local copies, waits for them, and re-layouts  1.26 us

profile of v6, /device:TPU:0, one launch (start us, length us, event | category | flops | bytes accessed | tf_op | source)
XLA Modules:
  0.0 29.0 jit_solution(12943846704555624851)
XLA Ops:
  0.6 27.1 %shard_map.77 = (bf16[64,128]{1,0:T(8,128)(2,1)S(1)}, f32[128,256]{1,0:T(8,128)S(1)}) custom-call(bf16[64,128]{1,0:T(8,128)(2,1)} %slab_hbm.1, bf16[1024,128]{1,0:T(8,128)(2,1)} %key_hbm.1, f32[1,128]{1,0:T(1,128)} %bitcast.1, bf16[1024,128]{1,0:T(8,128)(2,1)} %adj_hbm.1, f32[128,256]{1,0:T(8,128)} %cov_hbm.1, bf16[64,128]{1,0:T(8,128)(2,1)} %cot_hbm.1), custom_call_target="tpu_custom_call" | custom-call | tf_op jit(solution)/shard_map/pallas_call | solution.py:326
  27.8 0.6 %copy.10 = bf16[64,128]{1,0:T(8,128)(2,1)} copy(bf16[64,128]{1,0:T(8,128)(2,1)S(1)} %get-tuple-element.2) | data formatting | bytes 32768
  28.4 0.7 %copy.11 = f32[128,256]{1,0:T(8,128)} copy(f32[128,256]{1,0:T(8,128)S(1)} %get-tuple-element.3) | data formatting | bytes 262144

commit v7 on v6

--- a/solution.py
+++ b/solution.py
@@ -88,7 +88,7 @@
     def send_cot(q):
         own = cot.at[lab, chip]
         pltpu.make_async_remote_copy(
-            src_ref=own, dst_ref=own, send_sem=cot_send, recv_sem=cot_recv,
+            src_ref=own, dst_ref=own, send_sem=cot_send, recv_sem=cot_recv.at[g_me],
             device_id=(q, lab), device_id_type=MESH,
         ).start()
 
@@ -100,10 +100,14 @@
     loads[4].wait()
     send_cot(member(g_me, 1))
     lax.fori_loop(1, groups, send_cots, 0)
-    cot_copy = pltpu.make_async_remote_copy(
-        src_ref=cot.at[lab], dst_ref=cot.at[lab], send_sem=cot_pair_send,
-        recv_sem=cot_pair_recv, device_id=(me, other), device_id_type=MESH,
-    )
+
+    def cot_over(block):
+        pltpu.make_async_remote_copy(
+            src_ref=block, dst_ref=block, send_sem=cot_pair_send,
+            recv_sem=cot_pair_recv, device_id=(me, other), device_id_type=MESH,
+        ).start()
+
+    cot_over(cot.at[lab, chip])
 
     loads[0].wait()
     loads[1].wait()
@@ -164,17 +168,23 @@
 
         partial(group_at(k))
 
+        @pl.when(k == 0)
+        def _():
+            block = cot.at[lab, g_me * PAIR + lax.rem(chip + 1, PAIR)]
+            pltpu.make_async_copy(block, block, cot_recv.at[g_me]).wait()
+            cot_over(block)
+
         @pl.when(k > 0)
         def _():
+            block = cot.at[lab, pl.ds(group_at(k) * PAIR, PAIR)]
+            pltpu.make_async_copy(block, block, cot_recv.at[group_at(k)]).wait()
+            cot_over(block)
             g = group_at(k - 1)
             collect(g)
 
             @pl.when(k == 1)
             def _():
                 pltpu.make_async_copy(part.at[chip], got.at[chip], part_recv).start()
-                arrived = cot.at[lab, pl.ds(0, chips - 1)]
-                pltpu.make_async_copy(arrived, arrived, cot_recv).wait()
-                cot_copy.start()
 
             @pl.when(k > 1)
             def _():
@@ -189,7 +199,7 @@
     for j in range(PAIR):
         send_part(g, j)
 
-    cot_copy.wait()
+    pltpu.make_async_copy(cot.at[other], cot.at[other], cot_pair_recv).wait()
     sums_t = part[...].reshape(chips * rows, half).astype(jnp.float32).T.astype(jnp.bfloat16)
     for h in range(2):
         g_half = jnp.dot(
@@ -231,6 +241,21 @@
         lax.fori_loop(0, chunks, spread_some, 0)
         pl.when(me < chunks)(keep_grad)
 
+    def reduce_own():
+        pltpu.make_async_copy(ggot, ggot, g_recv).wait()
+        gall[me] = jnp.sum(ggot[...].astype(jnp.float32), axis=0).astype(jnp.bfloat16)
+
+        def fan(k, c):
+            send_fin(lax.rem(me + k, n))
+            return c
+
+        lax.fori_loop(1, n, fan, 0)
+
+    if n == chunks:
+        reduce_own()
+    else:
+        pl.when(me < chunks)(reduce_own)
+
     loads[3].wait()
     pltpu.make_async_copy(got, got, part_recv).wait()
     cross = jnp.sum(got[...].astype(jnp.float32), axis=0)
@@ -247,21 +272,6 @@
         device_id=(me, other), device_id_type=MESH,
     )
     mix_copy.start()
-
-    def reduce_own():
-        pltpu.make_async_copy(ggot, ggot, g_recv).wait()
-        gall[me] = jnp.sum(ggot[...].astype(jnp.float32), axis=0).astype(jnp.bfloat16)
-
-        def fan(k, c):
-            send_fin(lax.rem(me + k, n))
-            return c
-
-        lax.fori_loop(1, n, fan, 0)
-
-    if n == chunks:
-        reduce_own()
-    else:
-        pl.when(me < chunks)(reduce_own)
 
     mixed_own = mixed_part(lab)
     mix_copy.wait()
@@ -286,6 +296,7 @@
     rest = part.at[pl.ds(0, chips - 1)]
     pltpu.make_async_copy(rest, rest, part_send).wait()
     pltpu.make_async_copy(rest, rest, cot_send).wait()
+    pltpu.make_async_copy(cot.at[lab], cot.at[lab], cot_pair_send).wait()
     pltpu.make_async_copy(slab_all.at[0], slab_all.at[0], fwd_send).wait()
     pltpu.make_async_copy(pair_out, pair_out, pair_send).wait()
 
@@ -352,7 +363,7 @@
             pltpu.VMEM((1, keys), f32),
             dma((5,)), dma,
             dma, dma((groups,)), dma, dma((groups,)), dma, dma((groups,)),
-            *([dma] * 12),
+            *([dma] * 3), dma((groups,)), *([dma] * 8),
         ],
         compiler_params=pltpu.CompilerParams(
             collective_id=0, has_side_effects=True, vmem_limit_bytes=40 * 1024 * 1024

time: 29.3 us -> 29 us (0.990)
  no operation moved by 1% of the time
where the time goes in v7:
time: 29 us; the launch traced here: 28.8 us
  Pallas kernels  26.9 us (93%)
  local copies, waits for them, and re-layouts  1.26 us (4%)
  between operations  0.64 us (2%)
    pallas_call x1, Pallas kernels, local(): pl.pallas_call(functools.partial(kernel, n, chunks), out_shape=(pltpu.VME...  26.9 us
    unnamed x2, local copies, waits for them, and re-layouts  1.26 us

profile of v7, /device:TPU:0, one launch (start us, length us, event | category | flops | bytes accessed | tf_op | source)
XLA Modules:
  0.0 28.8 jit_solution(14588182271834829573)
XLA Ops:
  0.6 26.9 %shard_map.77 = (bf16[64,128]{1,0:T(8,128)(2,1)S(1)}, f32[128,256]{1,0:T(8,128)S(1)}) custom-call(bf16[64,128]{1,0:T(8,128)(2,1)} %slab_hbm.1, bf16[1024,128]{1,0:T(8,128)(2,1)} %key_hbm.1, f32[1,128]{1,0:T(1,128)} %bitcast.1, bf16[1024,128]{1,0:T(8,128)(2,1)} %adj_hbm.1, f32[128,256]{1,0:T(8,128)} %cov_hbm.1, bf16[64,128]{1,0:T(8,128)(2,1)} %cot_hbm.1), custom_call_target="tpu_custom_call" | custom-call | tf_op jit(solution)/shard_map/pallas_call | solution.py:337
  27.5 0.6 %copy.10 = bf16[64,128]{1,0:T(8,128)(2,1)} copy(bf16[64,128]{1,0:T(8,128)(2,1)S(1)} %get-tuple-element.2) | data formatting | bytes 32768
  28.1 0.7 %copy.11 = f32[128,256]{1,0:T(8,128)} copy(f32[128,256]{1,0:T(8,128)S(1)} %get-tuple-element.3) | data formatting | bytes 262144

commit v8 on v7

--- a/solution.py
+++ b/solution.py
@@ -159,12 +159,13 @@
     near = slab_all.at[core, g_me * PAIR + lax.rem(chip + 1, PAIR)]
     pltpu.make_async_copy(near, near, slab_recv.at[g_me]).wait()
     to_sibling(near, g_me)
+    forward(group_at(1))
     loads[2].wait()
 
     def step(k, c):
-        @pl.when(k + 1 < groups)
-        def _():
-            forward(group_at(k + 1))
+        @pl.when(k + 2 < groups)
+        def _():
+            forward(group_at(k + 2))
 
         partial(group_at(k))
 

time: 29 us -> 29.6 us (1.021)
  Pallas kernels: 26.9 us -> 27.5 us
    pallas_call x1, Pallas kernels: 26.9 us -> 27.5 us  [local(): pl.pallas_call(functools.partial(kernel, n, chunks), out_shape=(pltpu.VME...]
where the time goes in v8:
time: 29.6 us; the launch traced here: 29.4 us
  Pallas kernels  27.5 us (93%)
  local copies, waits for them, and re-layouts  1.26 us (4%)
  between operations  0.64 us (2%)
    pallas_call x1, Pallas kernels, local(): pl.pallas_call(functools.partial(kernel, n, chunks), out_shape=(pltpu.VME...  27.5 us
    unnamed x2, local copies, waits for them, and re-layouts  1.26 us

profile of v8, /device:TPU:0, one launch (start us, length us, event | category | flops | bytes accessed | tf_op | source)
XLA Modules:
  0.0 29.4 jit_solution(4712600859751455929)
XLA Ops:
  0.6 27.5 %shard_map.77 = (bf16[64,128]{1,0:T(8,128)(2,1)S(1)}, f32[128,256]{1,0:T(8,128)S(1)}) custom-call(bf16[64,128]{1,0:T(8,128)(2,1)} %slab_hbm.1, bf16[1024,128]{1,0:T(8,128)(2,1)} %key_hbm.1, f32[1,128]{1,0:T(1,128)} %bitcast.1, bf16[1024,128]{1,0:T(8,128)(2,1)} %adj_hbm.1, f32[128,256]{1,0:T(8,128)} %cov_hbm.1, bf16[64,128]{1,0:T(8,128)(2,1)} %cot_hbm.1), custom_call_target="tpu_custom_call" | custom-call | tf_op jit(solution)/shard_map/pallas_call | solution.py:338
  28.1 0.6 %copy.10 = bf16[64,128]{1,0:T(8,128)(2,1)} copy(bf16[64,128]{1,0:T(8,128)(2,1)S(1)} %get-tuple-element.2) | data formatting | bytes 32768
  28.7 0.7 %copy.11 = f32[128,256]{1,0:T(8,128)} copy(f32[128,256]{1,0:T(8,128)S(1)} %get-tuple-element.3) | data formatting | bytes 262144
